TPU v7x, 128 devices: a whole 4x4x4 slice. The times are simulated.
128 devices in a mesh: rows: 32 (over y, z, core), sub: 4 (over x).
Axes of the slice: x: 4, y: 4, z: 4, core: 2. Of those that a mesh axis runs over, the one named last changes fastest.
Arguments:
- windows: bfloat16 [2097152, 512], P(('rows', 'sub')), may hold values from -7 to 7
- landmark_index: int32 [512], replicated, may hold values from 0 to 2097151, as said below
- start_basis: float32 [512, 64], replicated, may hold values from -6 to 6
Outputs:
- embedding: float32 [64, 2097152], P(None, ('rows', 'sub'))
- basis: float32 [512, 64], replicated
Inputs may be any that keep to these rules, and one draw needn't show every extreme that they name: `landmark_index`: both the first and the last window are named in every draw.
All inputs are finite; a program needn't handle non-finite values.
Results may differ from a plain program's by a relative error of at most 0.0021.
Values sent between devices are 32-bit elements; how exact they have to be, the bound alone decides.
No kernel may reach another device: no remote copies, remote signals or barrier semaphores. Data moves between devices by JAX's collectives and lax.ppermute only.
A program may use at most 128 MiB of HBM per device.

v0:
```python
import jax
import jax.numpy as jnp
from jax import lax
from jax.sharding import PartitionSpec as P

ITERS = 8


sharpness = 6.0
epsilon = 1e-06


def inverse_norm(values):
    data = values.astype(jnp.float32)
    return lax.rsqrt(jnp.mean(data * data, axis=1) + epsilon)


def orthonormal(image):
    square = jnp.dot(image.T, image, precision=lax.Precision.HIGHEST)
    lower = jnp.linalg.cholesky(square)
    return jax.scipy.linalg.solve_triangular(lower, image.T, lower=True).T


def per_device(windows, landmark_index, start_basis):
    rows_here = windows.shape[0]
    width = windows.shape[1]
    position = lax.axis_index(("rows", "sub"))
    offset = position * rows_here
    shifted = landmark_index - offset
    inside = (shifted >= 0) & (shifted < rows_here)
    picked = jnp.take(windows, jnp.clip(shifted, 0, rows_here - 1), axis=0).astype(jnp.float32)
    picked = picked * inside[:, None].astype(jnp.float32)
    gathered = lax.psum(picked, ("rows", "sub"))
    land_inverse = inverse_norm(gathered)
    landmarks = gathered.astype(jnp.bfloat16)
    products = jnp.dot(windows, landmarks.T, preferred_element_type=jnp.float32)
    cosine = products * inverse_norm(windows)[:, None] * land_inverse[None, :] / width
    affinity = jnp.exp(sharpness * cosine)
    row_degree = jnp.sum(affinity, axis=1)
    scaled = (affinity * lax.rsqrt(row_degree)[:, None]).astype(jnp.bfloat16)
    column_part = jnp.sum(affinity, axis=0)
    cross_part = lax.dot_general(
        scaled, scaled, (((0,), (0,)), ((), ())), preferred_element_type=jnp.float32
    )
    basis = start_basis
    cross, column_degree = lax.psum((cross_part, column_part), ("rows", "sub"))
    column_inverse = lax.rsqrt(column_degree)
    gram = cross * column_inverse[:, None] * column_inverse[None, :]
    for step in range(ITERS):
        basis = orthonormal(jnp.dot(gram, basis, precision=lax.Precision.HIGHEST))
    weighted = (basis * column_inverse[:, None]).astype(jnp.bfloat16)
    embedding = lax.dot_general(
        weighted, scaled, (((0,), (1,)), ((), ())), preferred_element_type=jnp.float32
    )
    return (embedding, basis)


def solution(mesh):
    placed = (P(("rows", "sub"), None), P(), P())
    return jax.shard_map(
        per_device,
        mesh=mesh,
        in_specs=placed,
        out_specs=(P(None, ("rows", "sub")), P()),
        check_vma=False,
    )
```

profile of v0, /device:TPU:1, one launch (start us, length us, event | category | flops | bytes accessed | tf_op | source)
XLA Modules:
  0.0 517.7 jit_solution(980145019515674319)
XLA Ops:
  7.9 9.9 %gather_fusion = bf16[512,512]{1,0:T(8,128)(2,1)S(1)} fusion(bf16[16384,512]{1,0:T(8,128)(2,1)} %param.6, s32[1024]{0:T(1024)S(1)} %pad_clamp_fusion), kind=kCustom, calls=%fused_computation | custom fusion | bytes 1050624 | tf_op jit(solution)/shard_map/jit(_take)/gather | solution.py:31
  19.1 7.2 %multiply_reduce_fusion = f32[16384]{0:T(1024)S(1)} fusion(bf16[16384,512]{1,0:T(8,128)(2,1)} %param.6), kind=kLoop, calls=%fused_computation.3 | loop fusion | flops 25149440 | bytes 16842752 | tf_op jit(solution)/shard_map/reduce_sum | solution.py:15
  26.3 143.4 %all-reduce.3.cloned.1.call-done = f32[512,512]{1,0:T(8,128)} async-done(((f32[512,512]{1,0:T(8,128)}), f32[512,512]{1,0:T(8,128)}) %all-reduce.3.cloned.1.call-update) | async-done | bytes 1048592 | tf_op jit(solution)/shard_map/psum | solution.py:33
  171.2 21.1 %fusion.65 = (f32[512]{0:T(512)S(1)}, f32[16384]{0:T(1024)S(1)}, f32[512,16384]{1,0:T(8,128)}) fusion(f32[512]{0:T(512)S(1)} %add_rsqrt_fusion.1, f32[16384]{0:T(1024)S(1)} %add_rsqrt_fusion, bf16[16384,512]{1,0:T(8,128)(2,1)} %param.6, f32[512,512]{1,0:T(8,128)} %all-reduce.3.cloned.1.call-done), kind=kOutput, calls=%fused_computation.107 | convolution fusion | flops 8632123392 | bytes 51515392 | tf_op jit(solution)/shard_map/dot_general | solution.py:36
  192.3 23.8 %fusion = f32[512,512]{1,0:T(8,128)} fusion(f32[512,16384]{1,0:T(8,128)} %get-tuple-element.9, f32[16384]{0:T(1024)S(1)} %rsqrt.26), kind=kOutput, calls=%fused_computation.4 | convolution fusion | flops 8606711808 | bytes 34668544 | tf_op jit(solution)/shard_map/dot_general | solution.py:42
  216.1 65.0 %psum.23 = f32[512]{0:T(512)S(1)} all-reduce(f32[512]{0:T(512)S(1)} %get-tuple-element.4), channel_id=1, replica_groups=mesh['rows'=32,'sub'=4] {'rows','sub'}, use_global_device_ids=true, to_apply=%region_6.7 | all-reduce | flops 512 | bytes 4096 | tf_op jit(solution)/shard_map/psum | solution.py:46
  281.1 81.3 %all-reduce.5.cloned.1.call-done = f32[512,512]{1,0:T(8,128)} async-done(((f32[512,512]{1,0:T(8,128)}), f32[512,512]{1,0:T(8,128)}) %all-reduce.5.cloned.1.call-update) | async-done | bytes 1048592 | tf_op jit(solution)/shard_map/psum | solution.py:46
  365.3 5.8 %cholesky.134 = f32[64,64]{1,0:T(8,128)S(1)} custom-call(f32[64,64]{1,0:T(8,128)S(1)} %fusion.42), custom_call_target="Cholesky" | custom-call | tf_op jit(solution)/shard_map/jit(cholesky)/cholesky | solution.py:20
  372.5 4.9 custom-call.12
  377.7 2.5 fusion.63
  380.6 5.8 %cholesky.145 = f32[64,64]{1,0:T(8,128)S(1)} custom-call(f32[64,64]{1,0:T(8,128)S(1)} %fusion.40), custom_call_target="Cholesky" | custom-call | tf_op jit(solution)/shard_map/jit(cholesky)/cholesky | solution.py:20
  387.7 4.9 custom-call.13
  393.0 2.5 fusion.62
  395.8 5.8 %cholesky.156 = f32[64,64]{1,0:T(8,128)S(1)} custom-call(f32[64,64]{1,0:T(8,128)S(1)} %fusion.38), custom_call_target="Cholesky" | custom-call | tf_op jit(solution)/shard_map/jit(cholesky)/cholesky | solution.py:20
  403.0 4.9 custom-call.14
  408.3 2.5 fusion.61
  411.1 5.8 %cholesky.167 = f32[64,64]{1,0:T(8,128)S(1)} custom-call(f32[64,64]{1,0:T(8,128)S(1)} %fusion.36), custom_call_target="Cholesky" | custom-call | tf_op jit(solution)/shard_map/jit(cholesky)/cholesky | solution.py:20
  418.3 4.9 custom-call.15
  423.2 10.6 %fusion.10 = f32[64,512]{1,0:T(8,128)S(1)} fusion(f32[512,64]{0,1:T(8,128)S(1)} %fusion.61, f32[1,64,64]{1,2,0:T(8,128)S(1)} %custom-call.15), kind=kOutput, calls=%fused_computation.18 | convolution fusion | flops 25165824 | bytes 278528 | tf_op jit(solution)/shard_map/jit(_solve_triangular)/triangular_solve | solution.py:21
  433.8 2.5 fusion.60
  436.6 5.8 %cholesky.178 = f32[64,64]{1,0:T(8,128)S(1)} custom-call(f32[64,64]{1,0:T(8,128)S(1)} %fusion.34), custom_call_target="Cholesky" | custom-call | tf_op jit(solution)/shard_map/jit(cholesky)/cholesky | solution.py:20
  443.8 4.9 custom-call.16
  449.1 2.5 fusion.59
  451.9 5.8 %cholesky.189 = f32[64,64]{1,0:T(8,128)S(1)} custom-call(f32[64,64]{1,0:T(8,128)S(1)} %fusion.32), custom_call_target="Cholesky" | custom-call | tf_op jit(solution)/shard_map/jit(cholesky)/cholesky | solution.py:20
  459.1 4.9 custom-call.17
  464.4 2.5 fusion.58
  467.2 5.8 %cholesky.200 = f32[64,64]{1,0:T(8,128)S(1)} custom-call(f32[64,64]{1,0:T(8,128)S(1)} %fusion.30), custom_call_target="Cholesky" | custom-call | tf_op jit(solution)/shard_map/jit(cholesky)/cholesky | solution.py:20
  474.4 4.9 custom-call.18
  479.6 2.5 fusion.57
  482.5 5.8 %cholesky.211 = f32[64,64]{1,0:T(8,128)S(1)} custom-call(f32[64,64]{1,0:T(8,128)S(1)} %fusion.28), custom_call_target="Cholesky" | custom-call | tf_op jit(solution)/shard_map/jit(cholesky)/cholesky | solution.py:20
  489.7 4.9 custom-call.19
  494.9 15.7 %fusion.1 = f32[64,16384]{1,0:T(8,128)} fusion(f32[512,16384]{1,0:T(8,128)} %get-tuple-element.9, f32[16384]{0:T(1024)S(1)} %rsqrt.26, f32[512,64]{0,1:T(8,128)S(1)} %convolution_bitcast_fusion, f32[512]{0:T(512)S(1)} %rsqrt.27), kind=kOutput, calls=%fused_computation.5 | convolution fusion | flops 1090584576 | bytes 37947392 | tf_op jit(solution)/shard_map/dot_general | solution.py:52
  (72 shorter events, 21.6 us)
Async XLA Ops:
  7.2 355.3 %copy-start = (f32[512,64]{0,1:T(8,128)S(1)}, f32[512,64]{0,1:T(8,128)}, u32[]{:S(2)}) copy-start(f32[512,64]{0,1:T(8,128)} %param.8) | copy-start | bytes 393220
  7.2 162.6 %all-reduce.3.cloned.1.call-start = ((), (), s32[]{:S(2)}) async-start(), calls=%async_computation | async-start | bytes 2097152 | tf_op jit(solution)/shard_map/psum | solution.py:33
  19.1 343.4 %all-reduce.5.cloned.1.call-start = ((), (), s32[]{:S(2)}) async-start(), calls=%async_computation.1 | async-start | bytes 2097152 | tf_op jit(solution)/shard_map/psum | solution.py:46
  494.9 15.7 %copy-start.1 = (f32[512,64]{0,1:T(8,128)}, f32[512,64]{0,1:T(8,128)S(1)}, u32[]{:S(2)}) copy-start(f32[512,64]{0,1:T(8,128)S(1)} %convolution_bitcast_fusion) | copy-start | bytes 393220
Sparse Core Ops, SparseCore 0:
  19.2 150.5 all-reduce.2
  216.2 146.1 all-reduce.4
where the time goes:
time: 521 us; the launch traced here: 518 us
  waiting for transfers between devices  225 us (43%)
  other arithmetic  107 us (21%)
  matrix products  95.6 us (18%)
  blocking collectives  65 us (12%)
  between operations  14.6 us (3%)
  local copies, waits for them, and re-layouts  10.5 us (2%)
    psum x1, waiting for transfers between devices, per_device(): gathered = lax.psum(picked, ('rows', 'sub'))  143 us
    psum x1, waiting for transfers between devices, per_device(): cross, column_degree = lax.psum((cross_part, column_part), ('rows', 'sub'))  81.3 us
    psum x1, blocking collectives, per_device(): cross, column_degree = lax.psum((cross_part, column_part), ('rows', 'sub'))  65 us
    another operation x24, other arithmetic, orthonormal(): lower = jnp.linalg.cholesky(square)  52.2 us
    another operation x16, other arithmetic, orthonormal(): return jax.scipy.linalg.solve_triangular(lower, image.T, lower=True).T  44.4 us
    dot_general x1, matrix products, per_device(): lax.dot_general(scaled, scaled, (((0,), (0,)), ((), ())), preferred_eleme...  23.8 us
    dot_general x1, matrix products, per_device(): products = jnp.dot(windows, landmarks.T, preferred_element_type=jnp.float32)  21.1 us
    dot_general x8, matrix products, per_device(): basis = orthonormal(jnp.dot(gram, basis, precision=lax.Precision.HIGHEST))  20 us
  transfers between devices with their start and end apart: 2, of which 2 were waited for; matrix products, arithmetic and copies ran while one was open for 1% of the time, Pallas kernels for 0%

commit v1 on v0

v1 whole, which is shorter than its diff:
```python
import functools

import jax
import jax.numpy as jnp
import numpy as np
from jax import lax
from jax.experimental import pallas as pl
from jax.experimental.pallas import tpu as pltpu
from jax.sharding import PartitionSpec as P

ITERS = 8
BLOCK = 2048
SUB = 512
LANES = 128
CHUNK = 16

sharpness = 6.0
epsilon = 1e-06
LOG2E = 1.4426950408889634
HIGHEST = lax.Precision.HIGHEST


def dot(a, b, dims, precision=None):
    return lax.dot_general(
        a, b, (dims, ((), ())), precision=precision, preferred_element_type=jnp.float32
    )


NN = ((1,), (0,))
NT = ((1,), (1,))


def pick_kernel(shifted, windows, out, held, sem):
    count = shifted.shape[0]
    rows_here, width = windows.shape
    parts = width // LANES
    out[...] = jnp.zeros_like(out)

    def block_copy(j):
        start = pl.multiple_of((shifted[j] // 16) * 16, 16)
        return pltpu.make_async_copy(
            windows.at[pl.ds(start, 16), :], held.at[j], sem
        )

    def inside(j):
        return (shifted[j] >= 0) & (shifted[j] < rows_here)

    def begin(j, carry):
        @pl.when(inside(j))
        def _():
            block_copy(j).start()

        return carry

    def finish(j, carry):
        @pl.when(inside(j))
        def _():
            block_copy(j).wait()

        return carry

    def place(j, carry):
        @pl.when(inside(j))
        def _():
            block = held[j].astype(jnp.float32)
            row = lax.broadcasted_iota(jnp.int32, block.shape, 0)
            row = jnp.sum(jnp.where(row == shifted[j] % 16, block, 0.0), axis=0, keepdims=True)
            for c in range(parts):
                out[pl.ds(parts * j + c, 1), :] = row[:, c * LANES : (c + 1) * LANES]

        return carry

    lax.fori_loop(0, count, begin, 0, unroll=8)
    lax.fori_loop(0, count, finish, 0, unroll=8)
    lax.fori_loop(0, count, place, 0)


def pick(shifted, windows):
    count, width = shifted.shape[0], windows.shape[1]
    return pl.pallas_call(
        pick_kernel,
        out_shape=jax.ShapeDtypeStruct((count * width // LANES, LANES), jnp.float32),
        in_specs=[
            pl.BlockSpec(memory_space=pltpu.SMEM),
            pl.BlockSpec(memory_space=pl.ANY),
        ],
        out_specs=pl.BlockSpec(memory_space=pltpu.VMEM),
        scratch_shapes=[
            pltpu.VMEM((count, 16, width), jnp.bfloat16),
            pltpu.SemaphoreType.DMA,
        ],
        compiler_params=pltpu.CompilerParams(vmem_limit_bytes=32 * 2**20),
    )(shifted, windows)


def main_kernel(marks, windows, scaled, packed, land, land_scale, cross, column):
    step = pl.program_id(0)
    count, width = land.shape
    half = count // 2
    parts = width // LANES

    @pl.when(step == 0)
    def _():
        square = jnp.zeros((count, 1), jnp.float32)
        for c in range(parts):
            piece = marks[pl.ds(c, count, stride=parts), :]
            land[:, c * LANES : (c + 1) * LANES] = piece.astype(jnp.bfloat16)
            square += jnp.sum(piece * piece, axis=1, keepdims=True)
        inverse = lax.rsqrt(square / width + epsilon)
        land_scale[...] = jnp.broadcast_to(
            inverse * (sharpness * LOG2E / width), land_scale.shape
        )
        cross[...] = jnp.zeros_like(cross)
        column[...] = jnp.zeros_like(column)

    for t in range(BLOCK // SUB):
        part = slice(t * SUB, (t + 1) * SUB)
        data = windows[part, :]
        products = dot(land[...], data, NT)
        wide = data.astype(jnp.float32)
        mean = jnp.sum(wide * wide, axis=1, keepdims=True) / width
        inverse = jnp.transpose(jnp.broadcast_to(lax.rsqrt(mean + epsilon), (SUB, LANES)))[:1]
        scale = jnp.concatenate([land_scale[...]] * (SUB // LANES), axis=1)
        affinity = jnp.exp2(products * scale * inverse)
        total = jnp.sum(affinity, axis=0, keepdims=True)
        lanes = affinity[:, :LANES]
        for c in range(1, SUB // LANES):
            lanes += affinity[:, c * LANES : (c + 1) * LANES]
        column[...] += lanes
        rounded = (affinity * lax.rsqrt(total)).astype(jnp.bfloat16)
        scaled[:, part] = rounded
        low, high = rounded[:half], rounded[half:]
        cross[0] += dot(low, low, NT)
        cross[1] += dot(high, low, NT)
        cross[2] += dot(high, high, NT)

    @pl.when(step == pl.num_programs(0) - 1)
    def _():
        packed[...] = jnp.zeros_like(packed)
        at = 0
        for b in range(3):
            for c in range(half // LANES):
                packed[at : at + half, :] = cross[b, :, c * LANES : (c + 1) * LANES]
                at += half
        for c in range(count // LANES):
            turned = jnp.transpose(column[c * LANES : (c + 1) * LANES, :])
            packed[at : at + 1, :] = jnp.sum(turned, axis=0, keepdims=True)
            at += 1


def main_pass(marks, windows, total_rows):
    rows_here, width = windows.shape
    count = marks.shape[0] * LANES // width
    half = count // 2
    return pl.pallas_call(
        main_kernel,
        grid=(rows_here // BLOCK,),
        out_shape=(
            jax.ShapeDtypeStruct((count, rows_here), jnp.bfloat16),
            jax.ShapeDtypeStruct((total_rows, LANES), jnp.float32),
        ),
        in_specs=[
            pl.BlockSpec(marks.shape, lambda i: (0, 0)),
            pl.BlockSpec((BLOCK, width), lambda i: (i, 0)),
        ],
        out_specs=(
            pl.BlockSpec((count, BLOCK), lambda i: (0, i)),
            pl.BlockSpec((total_rows, LANES), lambda i: (0, 0)),
        ),
        scratch_shapes=[
            pltpu.VMEM((count, width), jnp.bfloat16),
            pltpu.VMEM((count, LANES), jnp.float32),
            pltpu.VMEM((3, half, half), jnp.float32),
            pltpu.VMEM((count, LANES), jnp.float32),
        ],
        compiler_params=pltpu.CompilerParams(
            dimension_semantics=("arbitrary",), vmem_limit_bytes=48 * 2**20
        ),
    )(marks, windows)


def inverse_cholesky(square):
    size = square.shape[0]
    row = lax.broadcasted_iota(jnp.int32, (size, 2 * size), 0)
    lane = lax.broadcasted_iota(jnp.int32, (size, 2 * size), 1)
    table = jnp.concatenate([square, jnp.zeros_like(square)], axis=1)
    table = jnp.where(lane == row + size, 1.0, table)
    pivots = jnp.zeros((size, 1), jnp.float32)
    for k in range(size):
        pivot_row = table[k : k + 1, :]
        column = table[:, k : k + 1]
        pivot = table[k : k + 1, k : k + 1]
        factor = jnp.where(row[:, :1] > k, column / pivot, 0.0)
        pivots = jnp.where(row[:, :1] == k, pivot, pivots)
        table = table - factor * pivot_row
    return table[:, size:] * lax.rsqrt(pivots)


def embed_kernel(packed, start, scaled, embedding, basis, gram, held, staged, in_sem, out_sem):
    count = gram.shape[0]
    half = count // 2
    blocks = held.shape[0]
    block = held.shape[2]
    reads = [
        pltpu.make_async_copy(
            scaled.at[:, pl.ds(b * block, block)], held.at[b], in_sem.at[b]
        )
        for b in range(blocks)
    ]
    for read in reads:
        read.start()

    base = 3 * half * (half // LANES)
    degree = jnp.concatenate(
        [packed[base + c : base + c + 1, :] for c in range(count // LANES)], axis=1
    )
    across = lax.rsqrt(degree)
    down = jnp.concatenate(
        [
            jnp.transpose(
                jnp.broadcast_to(across[:, c * LANES : (c + 1) * LANES], (LANES, LANES))
            )
            for c in range(count // LANES)
        ],
        axis=0,
    )

    def corner(b):
        at = b * half * (half // LANES)
        return jnp.concatenate(
            [packed[at + c * half : at + (c + 1) * half, :] for c in range(half // LANES)],
            axis=1,
        )

    wide = jnp.concatenate([down[:, :1]] * 1, axis=1)
    low = corner(0) * wide[:half] * across[:, :half]
    side = corner(1) * wide[half:] * across[:, :half]
    high = corner(2) * wide[half:] * across[:, half:]
    gram[:half, :half] = low
    gram[half:, :half] = side
    gram[:half, half:] = jnp.transpose(side)
    gram[half:, half:] = high

    def iterate(_, turned):
        image = dot(turned, gram[...], NN, HIGHEST)
        square = dot(image, image, NT, HIGHEST)
        return dot(inverse_cholesky(square), image, NN, HIGHEST)

    turned = lax.fori_loop(0, ITERS, iterate, jnp.transpose(start[...]))
    basis[...] = jnp.transpose(turned)
    weighted = (turned * across).astype(jnp.bfloat16)
    writes = []
    for b in range(blocks):
        reads[b].wait()
        staged[:, b * block : (b + 1) * block] = dot(weighted, held[b], NN)
        write = pltpu.make_async_copy(
            staged.at[:, pl.ds(b * block, block)],
            embedding.at[:, pl.ds(b * block, block)],
            out_sem.at[b],
        )
        write.start()
        writes.append(write)
    for write in writes:
        write.wait()


def embed(packed, start_basis, scaled):
    count, rows_here = scaled.shape
    kept = start_basis.shape[1]
    block = BLOCK
    blocks = rows_here // block
    return pl.pallas_call(
        embed_kernel,
        out_shape=(
            jax.ShapeDtypeStruct((kept, rows_here), jnp.float32),
            jax.ShapeDtypeStruct((count, kept), jnp.float32),
        ),
        in_specs=[
            pl.BlockSpec(memory_space=pltpu.VMEM),
            pl.BlockSpec(memory_space=pltpu.VMEM),
            pl.BlockSpec(memory_space=pl.ANY),
        ],
        out_specs=(
            pl.BlockSpec(memory_space=pl.ANY),
            pl.BlockSpec(memory_space=pltpu.VMEM),
        ),
        scratch_shapes=[
            pltpu.VMEM((count, count), jnp.float32),
            pltpu.VMEM((blocks, count, block), jnp.bfloat16),
            pltpu.VMEM((kept, rows_here), jnp.float32),
            pltpu.SemaphoreType.DMA((blocks,)),
            pltpu.SemaphoreType.DMA((blocks,)),
        ],
        compiler_params=pltpu.CompilerParams(vmem_limit_bytes=48 * 2**20),
    )(packed, start_basis, scaled)


def total_over(values, axes, devices):
    rows = values.shape[0] // devices
    pieces = values.reshape(devices, rows, LANES)
    pieces = lax.all_to_all(pieces, axes, 0, 0, tiled=True)
    mine = jnp.sum(pieces, axis=0)
    spread = jnp.broadcast_to(mine[None], pieces.shape)
    spread = lax.all_to_all(spread, axes, 0, 0, tiled=True)
    return spread.reshape(values.shape)


def per_device(devices, windows, landmark_index, start_basis):
    axes = ("rows", "sub")
    rows_here = windows.shape[0]
    shifted = landmark_index - lax.axis_index(axes) * rows_here
    marks = total_over(pick(shifted, windows), axes, devices)
    scaled, packed = main_pass(marks, windows, devices * CHUNK)
    packed = total_over(packed, axes, devices)
    return embed(packed, start_basis, scaled)


def solution(mesh):
    placed = (P(("rows", "sub"), None), P(), P())
    devices = int(np.prod(list(mesh.shape.values())))
    return jax.shard_map(
        functools.partial(per_device, devices),
        mesh=mesh,
        in_specs=placed,
        out_specs=(P(None, ("rows", "sub")), P()),
        check_vma=False,
    )
```

time: 521 us -> 220 us (0.42)
  waiting for transfers between devices: 225 us -> 19.8 us
  Pallas kernels: 0 us -> 110 us
  other arithmetic: 107 us -> 0.96 us
  matrix products: 95.6 us -> 0 us
  between operations: 14.6 us -> 0.7 us
  blocking collectives: 65 us -> 77 us
    psum x2 -> x0, waiting for transfers between devices: 225 us -> none  [the longest x1 143 us: per_device(): gathered = lax.psum(picked, ('rows', 'sub'))]
    pallas_call x0 -> x3, Pallas kernels: none -> 110 us  [the longest x1 62.7 us: embed(): pl.pallas_call(embed_kernel, out_shape=(jax.ShapeDtypeStruct((kept, rows_...]
    another operation x40 -> x0, other arithmetic: 96.5 us -> none  [the longest x24 52.2 us: orthonormal(): lower = jnp.linalg.cholesky(square)]
    dot_general x19 -> x0, matrix products: 82.6 us -> none  [the longest x1 23.8 us: per_device(): lax.dot_general(scaled, scaled, (((0,), (0,)), ((), ())), preferred_eleme...]
    all_to_all x0 -> x3, blocking collectives: none -> 77 us  [the longest x2 54 us: total_over(): pieces = lax.all_to_all(pieces, axes, 0, 0, tiled=True)]
    psum x1 -> x0, blocking collectives: 65 us -> none  [per_device(): cross, column_degree = lax.psum((cross_part, column_part), ('rows', 'sub'))]
    all_to_all x0 -> x1, waiting for transfers between devices: none -> 19.8 us  [total_over(): spread = lax.all_to_all(spread, axes, 0, 0, tiled=True)]
    another operation x8 -> x0, matrix products: 12.9 us -> none  [orthonormal(): return jax.scipy.linalg.solve_triangular(lower, image.T, lower=True).T]
  transfers between devices with their start and end apart: 2 -> 1, of which waited for: 2 -> 1; matrix products, arithmetic and copies ran while one was open for 1% -> 0% of each run, Pallas kernels for 0% -> 0%
where the time goes in v1:
time: 220 us; the launch traced here: 219 us
  Pallas kernels  110 us (50%)
  blocking collectives  77 us (35%)
  waiting for transfers between devices  19.8 us (9%)
  local copies, waits for them, and re-layouts  7.78 us (4%)
  starting transfers between devices  3.66 us (2%)
    pallas_call x1, Pallas kernels, embed(): pl.pallas_call(embed_kernel, out_shape=(jax.ShapeDtypeStruct((kept, rows_...  62.7 us
    all_to_all x2, blocking collectives, total_over(): pieces = lax.all_to_all(pieces, axes, 0, 0, tiled=True)  54 us
    pallas_call x1, Pallas kernels, main_pass(): pl.pallas_call(main_kernel, grid=(rows_here // BLOCK,), out_shape=(jax.Sh...  30.5 us
    all_to_all x1, blocking collectives, total_over(): spread = lax.all_to_all(spread, axes, 0, 0, tiled=True)  22.9 us
    all_to_all x1, waiting for transfers between devices, total_over(): spread = lax.all_to_all(spread, axes, 0, 0, tiled=True)  19.8 us
    pallas_call x1, Pallas kernels, pick(): pl.pallas_call(pick_kernel, out_shape=jax.ShapeDtypeStruct((count * width...  16.3 us
    unnamed x5, local copies, waits for them, and re-layouts  5.9 us
  transfers between devices with their start and end apart: 1, of which 1 were waited for; matrix products, arithmetic and copies ran while one was open for 0% of the time, Pallas kernels for 0%

profile of v1, /device:TPU:1, one launch (start us, length us, event | category | flops | bytes accessed | tf_op | source)
XLA Modules:
  0.0 219.3 jit_solution(16482490938369702432)
XLA Ops:
  0.6 0.7 broadcast_subtract_fusion.shifted
  1.3 0.0 copy-start
  1.3 5.8 %copy-done = bf16[16384,512]{1,0:T(8,128)(2,1)S(1)} copy-done((bf16[16384,512]{1,0:T(8,128)(2,1)S(1)}, bf16[16384,512]{1,0:T(8,128)(2,1)}, u32[]{:S(2)}) %copy-start) | copy-done | bytes 16777240
  7.1 16.3 %shard_map.50 = f32[2048,128]{1,0:T(8,128)S(1)} custom-call(s32[512]{0:T(512)S(1)} %broadcast_subtract_fusion.shifted, bf16[16384,512]{1,0:T(8,128)(2,1)S(1)} %copy-done), custom_call_target="tpu_custom_call" | custom-call | tf_op jit(solution)/shard_map/pallas_call | solution.py:80
  23.4 0.0 copy-start.1
  23.4 31.1 %all_to_all.20 = f32[128,16,128]{2,1,0:T(8,128)S(1)} all-to-all(f32[128,16,128]{2,1,0:T(8,128)S(1)} %bitcast.6), channel_id=1, replica_groups=mesh['rows'=32,'sub'=4] {'rows','sub'}, dimensions={0} | all-to-all | bytes 2097152 | tf_op jit(solution)/shard_map/all_to_all | solution.py:301
  54.6 0.1 reduce_sum.18
  54.7 0.1 broadcast_in_dim.4
  54.8 22.9 %all_to_all.21 = f32[128,16,128]{2,1,0:T(8,128)S(1)} all-to-all(f32[128,16,128]{2,1,0:T(8,128)S(1)} %broadcast_in_dim.4), channel_id=1, replica_groups=mesh['rows'=32,'sub'=4] {'rows','sub'}, dimensions={0} | all-to-all | bytes 2097152 | tf_op jit(solution)/shard_map/all_to_all | solution.py:304
  77.7 30.5 %shard_map.51 = (bf16[512,16384]{1,0:T(8,128)(2,1)}, f32[2048,128]{1,0:T(8,128)S(1)}) custom-call(f32[2048,128]{1,0:T(8,128)S(1)} %bitcast.5, bf16[16384,512]{1,0:T(8,128)(2,1)} %windows.3), custom_call_target="tpu_custom_call" | custom-call | tf_op jit(solution)/shard_map/pallas_call | solution.py:155
  108.2 22.9 %all_to_all.22 = f32[128,16,128]{2,1,0:T(8,128)S(1)} all-to-all(f32[128,16,128]{2,1,0:T(8,128)S(1)} %bitcast.7), channel_id=1, replica_groups=mesh['rows'=32,'sub'=4] {'rows','sub'}, dimensions={0} | all-to-all | bytes 2097152 | tf_op jit(solution)/shard_map/all_to_all | solution.py:301
  131.1 0.1 reduce_sum.19
  131.3 1.0 broadcast_in_dim.5
  132.3 3.7 %all-to-all-start.3 = ((f32[128,16,128]{2,1,0:T(8,128)}), f32[128,16,128]{2,1,0:T(8,128)S(1)}, u32[]{:S(2)}, u32[]{:S(2)}) async-start(f32[128,16,128]{2,1,0:T(8,128)} %broadcast_in_dim.5), calls=%async_computation.3 | async-start | bytes 2097152 | tf_op jit(solution)/shard_map/all_to_all | solution.py:304
  136.0 0.0 copy-done.1
  136.0 0.1 copy.5.start
  136.1 19.8 %all-to-all-done.3 = f32[128,16,128]{2,1,0:T(8,128)S(1)} async-done(((f32[128,16,128]{2,1,0:T(8,128)}), f32[128,16,128]{2,1,0:T(8,128)S(1)}, u32[]{:S(2)}, u32[]{:S(2)}) %all-to-all-start.3) | async-done | bytes 1048608 | tf_op jit(solution)/shard_map/all_to_all | solution.py:304
  155.9 62.7 %shard_map.52 = (f32[64,16384]{1,0:T(8,128)}, f32[512,64]{1,0:T(8,128)S(1)}) custom-call(f32[2048,128]{1,0:T(8,128)S(1)} %bitcast.4, f32[512,64]{1,0:T(8,128)S(1)} %copy.5.start, bf16[512,16384]{1,0:T(8,128)(2,1)} %get-tuple-element.5.scaled), custom_call_target="tpu_custom_call" | custom-call | tf_op jit(solution)/shard_map/pallas_call | solution.py:272
  218.6 0.8 copy.6
Async XLA Ops:
  1.3 5.8 %copy-start = (bf16[16384,512]{1,0:T(8,128)(2,1)S(1)}, bf16[16384,512]{1,0:T(8,128)(2,1)}, u32[]{:S(2)}) copy-start(bf16[16384,512]{1,0:T(8,128)(2,1)} %windows.3) | copy-start | bytes 50331652
  23.4 112.5 %copy-start.1 = (f32[512,64]{0,1:T(8,128)S(1)}, f32[512,64]{0,1:T(8,128)}, u32[]{:S(2)}) copy-start(f32[512,64]{0,1:T(8,128)} %param.5) | copy-start | bytes 393220
  132.3 23.6 %all-to-all-start.3 = ((f32[128,16,128]{2,1,0:T(8,128)}), f32[128,16,128]{2,1,0:T(8,128)S(1)}, u32[]{:S(2)}, u32[]{:S(2)}) async-start(f32[128,16,128]{2,1,0:T(8,128)} %broadcast_in_dim.5), calls=%async_computation.3 | async-start | bytes 2097152 | tf_op jit(solution)/shard_map/all_to_all | solution.py:304

commit v2 on v1

--- a/solution.py
+++ b/solution.py
@@ -30,55 +30,51 @@
 NT = ((1,), (1,))
 
 
-def pick_kernel(shifted, windows, out, held, sem):
-    count = shifted.shape[0]
+def pick_kernel(axes, index, windows, out, held, listed, sem):
+    count = index.shape[0]
     rows_here, width = windows.shape
     parts = width // LANES
+    offset = lax.axis_index(axes) * rows_here
+
+    def note(j, found):
+        local = index[j] - offset
+        listed[found] = j
+        return found + ((local >= 0) & (local < rows_here)).astype(jnp.int32)
+
+    found = lax.fori_loop(0, count, note, 0, unroll=16)
+
+    def block_copy(n):
+        start = pl.multiple_of(((index[listed[n]] - offset) // 16) * 16, 16)
+        return pltpu.make_async_copy(windows.at[pl.ds(start, 16), :], held.at[n], sem)
+
+    def begin(n, carry):
+        block_copy(n).start()
+        return carry
+
+    def finish(n, carry):
+        block_copy(n).wait()
+        return carry
+
+    def place(n, carry):
+        j = listed[n]
+        block = held[n].astype(jnp.float32)
+        row = lax.broadcasted_iota(jnp.int32, block.shape, 0)
+        here = row == (index[j] - offset) % 16
+        row = jnp.sum(jnp.where(here, block, 0.0), axis=0, keepdims=True)
+        for c in range(parts):
+            out[pl.ds(parts * j + c, 1), :] = row[:, c * LANES : (c + 1) * LANES]
+        return carry
+
+    lax.fori_loop(0, found, begin, 0)
     out[...] = jnp.zeros_like(out)
-
-    def block_copy(j):
-        start = pl.multiple_of((shifted[j] // 16) * 16, 16)
-        return pltpu.make_async_copy(
-            windows.at[pl.ds(start, 16), :], held.at[j], sem
-        )
-
-    def inside(j):
-        return (shifted[j] >= 0) & (shifted[j] < rows_here)
-
-    def begin(j, carry):
-        @pl.when(inside(j))
-        def _():
-            block_copy(j).start()
-
-        return carry
-
-    def finish(j, carry):
-        @pl.when(inside(j))
-        def _():
-            block_copy(j).wait()
-
-        return carry
-
-    def place(j, carry):
-        @pl.when(inside(j))
-        def _():
-            block = held[j].astype(jnp.float32)
-            row = lax.broadcasted_iota(jnp.int32, block.shape, 0)
-            row = jnp.sum(jnp.where(row == shifted[j] % 16, block, 0.0), axis=0, keepdims=True)
-            for c in range(parts):
-                out[pl.ds(parts * j + c, 1), :] = row[:, c * LANES : (c + 1) * LANES]
-
-        return carry
-
-    lax.fori_loop(0, count, begin, 0, unroll=8)
-    lax.fori_loop(0, count, finish, 0, unroll=8)
-    lax.fori_loop(0, count, place, 0)
-
-
-def pick(shifted, windows):
-    count, width = shifted.shape[0], windows.shape[1]
+    lax.fori_loop(0, found, finish, 0)
+    lax.fori_loop(0, found, place, 0)
+
+
+def pick(index, windows, axes):
+    count, width = index.shape[0], windows.shape[1]
     return pl.pallas_call(
-        pick_kernel,
+        functools.partial(pick_kernel, axes),
         out_shape=jax.ShapeDtypeStruct((count * width // LANES, LANES), jnp.float32),
         in_specs=[
             pl.BlockSpec(memory_space=pltpu.SMEM),
@@ -87,10 +83,11 @@
         out_specs=pl.BlockSpec(memory_space=pltpu.VMEM),
         scratch_shapes=[
             pltpu.VMEM((count, 16, width), jnp.bfloat16),
+            pltpu.SMEM((count + 1,), jnp.int32),
             pltpu.SemaphoreType.DMA,
         ],
-        compiler_params=pltpu.CompilerParams(vmem_limit_bytes=32 * 2**20),
-    )(shifted, windows)
+        compiler_params=pltpu.CompilerParams(vmem_limit_bytes=56 * 2**20),
+    )(index, windows)
 
 
 def main_kernel(marks, windows, scaled, packed, land, land_scale, cross, column):
@@ -185,15 +182,25 @@
     lane = lax.broadcasted_iota(jnp.int32, (size, 2 * size), 1)
     table = jnp.concatenate([square, jnp.zeros_like(square)], axis=1)
     table = jnp.where(lane == row + size, 1.0, table)
-    pivots = jnp.zeros((size, 1), jnp.float32)
-    for k in range(size):
-        pivot_row = table[k : k + 1, :]
-        column = table[:, k : k + 1]
-        pivot = table[k : k + 1, k : k + 1]
-        factor = jnp.where(row[:, :1] > k, column / pivot, 0.0)
-        pivots = jnp.where(row[:, :1] == k, pivot, pivots)
-        table = table - factor * pivot_row
-    return table[:, size:] * lax.rsqrt(pivots)
+    done = []
+    for at in range(0, size, 8):
+        left = size - at
+        panel = [
+            jnp.broadcast_to(table[:, at + j : at + j + 1], (left, 2 * size))
+            for j in range(8)
+        ]
+        for j in range(8):
+            pivot = panel[j][j : j + 1]
+            pivot_row = table[j : j + 1]
+            factor = panel[j] * (1.0 / pivot)
+            first = jnp.where(row[:8] > j, factor[:8], 0.0)
+            factor = jnp.concatenate([first, factor[8:]], axis=0) if left > 8 else first
+            done.append((pivot_row * lax.rsqrt(pivot))[:, size:])
+            for q in range(j + 1, 8):
+                panel[q] -= factor * panel[q][j : j + 1]
+            table -= factor * pivot_row
+        table = table[8:]
+    return jnp.concatenate(done, axis=0)
 
 
 def embed_kernel(packed, start, scaled, embedding, basis, gram, held, staged, in_sem, out_sem):
@@ -247,7 +254,7 @@
         return dot(inverse_cholesky(square), image, NN, HIGHEST)
 
     turned = lax.fori_loop(0, ITERS, iterate, jnp.transpose(start[...]))
-    basis[...] = jnp.transpose(turned)
+    basis[...] = turned
     weighted = (turned * across).astype(jnp.bfloat16)
     writes = []
     for b in range(blocks):
@@ -273,7 +280,7 @@
         embed_kernel,
         out_shape=(
             jax.ShapeDtypeStruct((kept, rows_here), jnp.float32),
-            jax.ShapeDtypeStruct((count, kept), jnp.float32),
+            jax.ShapeDtypeStruct((kept, count), jnp.float32),
         ),
         in_specs=[
             pl.BlockSpec(memory_space=pltpu.VMEM),
@@ -307,12 +314,11 @@
 
 def per_device(devices, windows, landmark_index, start_basis):
     axes = ("rows", "sub")
-    rows_here = windows.shape[0]
-    shifted = landmark_index - lax.axis_index(axes) * rows_here
-    marks = total_over(pick(shifted, windows), axes, devices)
+    marks = total_over(pick(landmark_index, windows, axes), axes, devices)
     scaled, packed = main_pass(marks, windows, devices * CHUNK)
     packed = total_over(packed, axes, devices)
-    return embed(packed, start_basis, scaled)
+    embedding, turned = embed(packed, start_basis, scaled)
+    return embedding, turned.T
 
 
 def solution(mesh):

time: 220 us -> 168 us (0.76)
  Pallas kernels: 110 us -> 65 us
  local copies, waits for them, and re-layouts: 7.78 us -> 1.24 us
    pallas_call x1, Pallas kernels: 62.7 us -> 30.5 us  [embed(): pl.pallas_call(embed_kernel, out_shape=(jax.ShapeDtypeStruct((kept, rows_...]
    pallas_call x1, Pallas kernels: 16.3 us -> 4.12 us  [pick(): pl.pallas_call(functools.partial(pick_kernel, axes), out_shape=jax.ShapeD...]
    unnamed x5 -> x3, local copies, waits for them, and re-layouts: 5.9 us -> 0.13 us
where the time goes in v2:
time: 168 us
  blocking collectives  77.1 us (46%)
  Pallas kernels  65 us (39%)
  waiting for transfers between devices  19.8 us (12%)
  starting transfers between devices  3.66 us (2%)
    all_to_all x2, blocking collectives, total_over(): pieces = lax.all_to_all(pieces, axes, 0, 0, tiled=True)  54.2 us
    pallas_call x1, Pallas kernels, embed(): pl.pallas_call(embed_kernel, out_shape=(jax.ShapeDtypeStruct((kept, rows_...  30.5 us
    pallas_call x1, Pallas kernels, main_pass(): pl.pallas_call(main_kernel, grid=(rows_here // BLOCK,), out_shape=(jax.Sh...  30.4 us
    all_to_all x1, blocking collectives, total_over(): spread = lax.all_to_all(spread, axes, 0, 0, tiled=True)  22.9 us
    all_to_all x1, waiting for transfers between devices, total_over(): spread = lax.all_to_all(spread, axes, 0, 0, tiled=True)  19.8 us
    pallas_call x1, Pallas kernels, pick(): pl.pallas_call(functools.partial(pick_kernel, axes), out_shape=jax.ShapeD...  4.12 us
    all_to_all x1, starting transfers between devices, total_over(): spread = lax.all_to_all(spread, axes, 0, 0, tiled=True)  3.66 us
  transfers between devices with their start and end apart: 1, of which 1 were waited for; matrix products, arithmetic and copies ran while one was open for 0% of the time, Pallas kernels for 0%

profile of v2, /device:TPU:1, one launch (start us, length us, event | category | flops | bytes accessed | tf_op | source)
XLA Modules:
  0.0 167.7 jit_solution(900107799098850587)
XLA Ops:
  0.6 4.1 %shard_map.50 = f32[2048,128]{1,0:T(8,128)} custom-call(s32[512]{0:T(512)} %index.1, bf16[16384,512]{1,0:T(8,128)(2,1)} %windows.3), custom_call_target="tpu_custom_call" | custom-call | tf_op jit(solution)/shard_map/pallas_call | solution.py:76
  4.8 0.0 copy-start
  4.8 31.3 %all_to_all.20 = f32[128,16,128]{2,1,0:T(8,128)S(1)} all-to-all(f32[128,16,128]{2,1,0:T(8,128)} %bitcast.8), channel_id=1, replica_groups=mesh['rows'=32,'sub'=4] {'rows','sub'}, dimensions={0} | all-to-all | bytes 2097152 | tf_op jit(solution)/shard_map/all_to_all | solution.py:308
  36.0 0.1 reduce_sum.18
  36.2 0.1 broadcast_in_dim.4
  36.3 22.9 %all_to_all.21 = f32[128,16,128]{2,1,0:T(8,128)S(1)} all-to-all(f32[128,16,128]{2,1,0:T(8,128)S(1)} %broadcast_in_dim.4), channel_id=1, replica_groups=mesh['rows'=32,'sub'=4] {'rows','sub'}, dimensions={0} | all-to-all | bytes 2097152 | tf_op jit(solution)/shard_map/all_to_all | solution.py:311
  59.2 30.4 %shard_map.51 = (bf16[512,16384]{1,0:T(8,128)(2,1)}, f32[2048,128]{1,0:T(8,128)S(1)}) custom-call(f32[2048,128]{1,0:T(8,128)S(1)} %bitcast.6, bf16[16384,512]{1,0:T(8,128)(2,1)} %windows.3), custom_call_target="tpu_custom_call" | custom-call | tf_op jit(solution)/shard_map/pallas_call | solution.py:152
  89.6 22.9 %all_to_all.22 = f32[128,16,128]{2,1,0:T(8,128)S(1)} all-to-all(f32[128,16,128]{2,1,0:T(8,128)S(1)} %bitcast.7), channel_id=1, replica_groups=mesh['rows'=32,'sub'=4] {'rows','sub'}, dimensions={0} | all-to-all | bytes 2097152 | tf_op jit(solution)/shard_map/all_to_all | solution.py:308
  112.5 0.1 reduce_sum.19
  112.6 1.0 broadcast_in_dim.5
  113.7 3.7 %all-to-all-start.3 = ((f32[128,16,128]{2,1,0:T(8,128)}), f32[128,16,128]{2,1,0:T(8,128)S(1)}, u32[]{:S(2)}, u32[]{:S(2)}) async-start(f32[128,16,128]{2,1,0:T(8,128)} %broadcast_in_dim.5), calls=%async_computation.3 | async-start | bytes 2097152 | tf_op jit(solution)/shard_map/all_to_all | solution.py:311
  117.3 0.0 copy-done
  117.3 0.1 copy.5.start
  117.5 19.8 %all-to-all-done.3 = f32[128,16,128]{2,1,0:T(8,128)S(1)} async-done(((f32[128,16,128]{2,1,0:T(8,128)}), f32[128,16,128]{2,1,0:T(8,128)S(1)}, u32[]{:S(2)}, u32[]{:S(2)}) %all-to-all-start.3) | async-done | bytes 1048608 | tf_op jit(solution)/shard_map/all_to_all | solution.py:311
  137.2 30.5 %shard_map.52 = (f32[64,16384]{1,0:T(8,128)}, f32[64,512]{1,0:T(8,128)}) custom-call(f32[2048,128]{1,0:T(8,128)S(1)} %bitcast.5, f32[512,64]{1,0:T(8,128)S(1)} %copy.5.start, bf16[512,16384]{1,0:T(8,128)(2,1)} %get-tuple-element.7.scaled), custom_call_target="tpu_custom_call" | custom-call | tf_op jit(solution)/shard_map/pallas_call | solution.py:279
Async XLA Ops:
  4.8 112.6 %copy-start = (f32[512,64]{0,1:T(8,128)S(1)}, f32[512,64]{0,1:T(8,128)}, u32[]{:S(2)}) copy-start(f32[512,64]{0,1:T(8,128)} %param.5) | copy-start | bytes 393220
  113.7 23.6 %all-to-all-start.3 = ((f32[128,16,128]{2,1,0:T(8,128)}), f32[128,16,128]{2,1,0:T(8,128)S(1)}, u32[]{:S(2)}, u32[]{:S(2)}) async-start(f32[128,16,128]{2,1,0:T(8,128)} %broadcast_in_dim.5), calls=%async_computation.3 | async-start | bytes 2097152 | tf_op jit(solution)/shard_map/all_to_all | solution.py:311

commit v3 on v2

--- a/solution.py
+++ b/solution.py
@@ -9,8 +9,10 @@
 from jax.sharding import PartitionSpec as P
 
 ITERS = 8
-BLOCK = 2048
+GROUPS = ((2, 4e-6), (3, 4e-6), (3, 2e-2))
 SUB = 512
+UNROLL = 4
+ROWS = 16
 LANES = 128
 CHUNK = 16
 
@@ -90,90 +92,176 @@
     )(index, windows)
 
 
-def main_kernel(marks, windows, scaled, packed, land, land_scale, cross, column):
-    step = pl.program_id(0)
+def main_kernel(
+    marks, windows, scaled, packed, land, land_scale, held, made, products, cross, column, in_sem, out_sem
+):
     count, width = land.shape
     half = count // 2
     parts = width // LANES
-
-    @pl.when(step == 0)
-    def _():
-        square = jnp.zeros((count, 1), jnp.float32)
-        for c in range(parts):
-            piece = marks[pl.ds(c, count, stride=parts), :]
-            land[:, c * LANES : (c + 1) * LANES] = piece.astype(jnp.bfloat16)
-            square += jnp.sum(piece * piece, axis=1, keepdims=True)
-        inverse = lax.rsqrt(square / width + epsilon)
-        land_scale[...] = jnp.broadcast_to(
-            inverse * (sharpness * LOG2E / width), land_scale.shape
+    blocks = held.shape[0]
+
+    def read(b):
+        return pltpu.make_async_copy(
+            windows.at[pl.ds(b * SUB, SUB), :], held.at[b], in_sem.at[b]
         )
-        cross[...] = jnp.zeros_like(cross)
-        column[...] = jnp.zeros_like(column)
-
-    for t in range(BLOCK // SUB):
-        part = slice(t * SUB, (t + 1) * SUB)
-        data = windows[part, :]
-        products = dot(land[...], data, NT)
-        wide = data.astype(jnp.float32)
-        mean = jnp.sum(wide * wide, axis=1, keepdims=True) / width
-        inverse = jnp.transpose(jnp.broadcast_to(lax.rsqrt(mean + epsilon), (SUB, LANES)))[:1]
-        scale = jnp.concatenate([land_scale[...]] * (SUB // LANES), axis=1)
-        affinity = jnp.exp2(products * scale * inverse)
-        total = jnp.sum(affinity, axis=0, keepdims=True)
-        lanes = affinity[:, :LANES]
-        for c in range(1, SUB // LANES):
-            lanes += affinity[:, c * LANES : (c + 1) * LANES]
-        column[...] += lanes
-        rounded = (affinity * lax.rsqrt(total)).astype(jnp.bfloat16)
-        scaled[:, part] = rounded
-        low, high = rounded[:half], rounded[half:]
+
+    def write(b):
+        return pltpu.make_async_copy(made.at[b + 1], scaled.at[b], out_sem.at[b])
+
+    def begin(b, carry):
+        read(b).start()
+        return carry
+
+    lax.fori_loop(0, blocks, begin, 0)
+
+    square = jnp.zeros((count, 1), jnp.float32)
+    for c in range(parts):
+        piece = marks[pl.ds(c, count, stride=parts), :]
+        land[:, c * LANES : (c + 1) * LANES] = piece.astype(jnp.bfloat16)
+        square += jnp.sum(piece * piece, axis=1, keepdims=True)
+    inverse = lax.rsqrt(square / width + epsilon)
+    land_scale[...] = jnp.broadcast_to(
+        inverse * (sharpness * LOG2E / width), land_scale.shape
+    )
+    cross[...] = jnp.zeros_like(cross)
+    column[...] = jnp.zeros_like(column)
+    made[0] = jnp.zeros(made.shape[1:], made.dtype)
+
+    def multiply(b, slot):
+        products[slot] = dot(land[...], held[b], NT)
+
+    def window_scale(b):
+        lane = lax.broadcasted_iota(jnp.int32, (LANES, LANES), 1)
+        table = jnp.zeros((LANES, LANES), jnp.float32)
+        for g in range(SUB // LANES):
+            wide = held[b, g * LANES : (g + 1) * LANES, :].astype(jnp.float32)
+            wide = wide * wide
+            lanes = wide[:, :LANES]
+            for c in range(1, parts):
+                lanes += wide[:, c * LANES : (c + 1) * LANES]
+            mean = jnp.sum(lanes, axis=1, keepdims=True) / width
+            table = jnp.where(lane == g, mean, table)
+        table = jnp.transpose(table)[: SUB // LANES]
+        table = lax.rsqrt(table + epsilon)
+        return jnp.concatenate([table[g : g + 1] for g in range(SUB // LANES)], axis=1)
+
+    def shape(b, slot):
+        inverse = jnp.broadcast_to(window_scale(b), (ROWS, SUB))
+        total = jnp.zeros((8, SUB), jnp.float32)
+        for r in range(0, count, ROWS):
+            scale = jnp.concatenate([land_scale[r : r + ROWS, :]] * (SUB // LANES), axis=1)
+            affinity = jnp.exp2(products[slot, r : r + ROWS, :] * scale * inverse)
+            products[slot, r : r + ROWS, :] = affinity
+            for k in range(0, ROWS, 8):
+                total += affinity[k : k + 8]
+            lanes = affinity[:, :LANES]
+            for c in range(1, SUB // LANES):
+                lanes += affinity[:, c * LANES : (c + 1) * LANES]
+            column[r : r + ROWS, :] += lanes
+        root = lax.rsqrt(jnp.sum(total, axis=0, keepdims=True))
+        root = jnp.broadcast_to(root, (ROWS, SUB))
+        for r in range(0, count, ROWS):
+            made[b + 1, r : r + ROWS, :] = (products[slot, r : r + ROWS, :] * root).astype(
+                jnp.bfloat16
+            )
+
+    def gather(b):
+        low, high = made[b + 1, :half], made[b + 1, half:]
         cross[0] += dot(low, low, NT)
         cross[1] += dot(high, low, NT)
         cross[2] += dot(high, high, NT)
 
-    @pl.when(step == pl.num_programs(0) - 1)
-    def _():
-        packed[...] = jnp.zeros_like(packed)
-        at = 0
-        for b in range(3):
-            for c in range(half // LANES):
-                packed[at : at + half, :] = cross[b, :, c * LANES : (c + 1) * LANES]
-                at += half
-        for c in range(count // LANES):
-            turned = jnp.transpose(column[c * LANES : (c + 1) * LANES, :])
-            packed[at : at + 1, :] = jnp.sum(turned, axis=0, keepdims=True)
-            at += 1
+    read(0).wait()
+    multiply(0, 0)
+
+    def several(i, carry):
+        b = UNROLL * i
+        for k in range(1, UNROLL):
+            read(b + k).wait()
+
+        @pl.when(b + UNROLL < blocks)
+        def _():
+            read(b + UNROLL).wait()
+
+        for k in range(UNROLL):
+            following = b + k + 1 if k + 1 < UNROLL else jnp.minimum(b + UNROLL, blocks - 1)
+            gather(b + k - 1)
+            multiply(following, (k + 1) % 2)
+            shape(b + k, k % 2)
+        for k in range(UNROLL):
+            write(b + k).start()
+        return carry
+
+    lax.fori_loop(0, blocks // UNROLL, several, 0)
+    gather(blocks - 1)
+
+    packed[...] = jnp.zeros_like(packed)
+    at = 0
+    for b in range(3):
+        for c in range(half // LANES):
+            packed[at : at + half, :] = cross[b, :, c * LANES : (c + 1) * LANES]
+            at += half
+    for c in range(count // LANES):
+        turned = jnp.transpose(column[c * LANES : (c + 1) * LANES, :])
+        packed[at : at + 1, :] = jnp.sum(turned, axis=0, keepdims=True)
+        at += 1
+
+    def finish(b, carry):
+        write(b).wait()
+        return carry
+
+    lax.fori_loop(0, blocks, finish, 0)
 
 
 def main_pass(marks, windows, total_rows):
     rows_here, width = windows.shape
     count = marks.shape[0] * LANES // width
     half = count // 2
+    blocks = rows_here // SUB
     return pl.pallas_call(
         main_kernel,
-        grid=(rows_here // BLOCK,),
         out_shape=(
-            jax.ShapeDtypeStruct((count, rows_here), jnp.bfloat16),
+            jax.ShapeDtypeStruct((blocks, count, SUB), jnp.bfloat16),
             jax.ShapeDtypeStruct((total_rows, LANES), jnp.float32),
         ),
         in_specs=[
-            pl.BlockSpec(marks.shape, lambda i: (0, 0)),
-            pl.BlockSpec((BLOCK, width), lambda i: (i, 0)),
+            pl.BlockSpec(memory_space=pltpu.VMEM),
+            pl.BlockSpec(memory_space=pl.ANY),
         ],
         out_specs=(
-            pl.BlockSpec((count, BLOCK), lambda i: (0, i)),
-            pl.BlockSpec((total_rows, LANES), lambda i: (0, 0)),
+            pl.BlockSpec(memory_space=pl.ANY),
+            pl.BlockSpec(memory_space=pltpu.VMEM),
         ),
         scratch_shapes=[
             pltpu.VMEM((count, width), jnp.bfloat16),
             pltpu.VMEM((count, LANES), jnp.float32),
+            pltpu.VMEM((blocks, SUB, width), jnp.bfloat16),
+            pltpu.VMEM((blocks + 1, count, SUB), jnp.bfloat16),
+            pltpu.VMEM((2, count, SUB), jnp.float32),
             pltpu.VMEM((3, half, half), jnp.float32),
             pltpu.VMEM((count, LANES), jnp.float32),
-        ],
-        compiler_params=pltpu.CompilerParams(
-            dimension_semantics=("arbitrary",), vmem_limit_bytes=48 * 2**20
-        ),
+            pltpu.SemaphoreType.DMA((blocks,)),
+            pltpu.SemaphoreType.DMA((blocks,)),
+        ],
+        compiler_params=pltpu.CompilerParams(vmem_limit_bytes=44 * 2**20),
     )(marks, windows)
+
+
+def split(values):
+    high = values.astype(jnp.bfloat16)
+    rest = values - high.astype(jnp.float32)
+    middle = rest.astype(jnp.bfloat16)
+    low = (rest - middle.astype(jnp.float32)).astype(jnp.bfloat16)
+    return high, middle, low
+
+
+def exact_dot(a, b, dims):
+    n = a[0].shape[0]
+    high = dot(jnp.concatenate(a, axis=0), b[0], dims)
+    middle = dot(jnp.concatenate(a[:2], axis=0), b[1], dims)
+    low = dot(a[0], b[2], dims)
+    small = high[2 * n :] + middle[n:] + low
+    return high[:n] + (high[n : 2 * n] + middle[:n] + small)
 
 
 def inverse_cholesky(square):
@@ -181,8 +269,9 @@
     row = lax.broadcasted_iota(jnp.int32, (size, 2 * size), 0)
     lane = lax.broadcasted_iota(jnp.int32, (size, 2 * size), 1)
     table = jnp.concatenate([square, jnp.zeros_like(square)], axis=1)
+    diagonal = jnp.sum(jnp.where(lane == row, table, 0.0), axis=1, keepdims=True)
     table = jnp.where(lane == row + size, 1.0, table)
-    done = []
+    done, pivots = [], []
     for at in range(0, size, 8):
         left = size - at
         panel = [
@@ -196,26 +285,31 @@
             first = jnp.where(row[:8] > j, factor[:8], 0.0)
             factor = jnp.concatenate([first, factor[8:]], axis=0) if left > 8 else first
             done.append((pivot_row * lax.rsqrt(pivot))[:, size:])
+            pivots.append(pivot)
             for q in range(j + 1, 8):
                 panel[q] -= factor * panel[q][j : j + 1]
             table -= factor * pivot_row
         table = table[8:]
-    return jnp.concatenate(done, axis=0)
-
-
-def embed_kernel(packed, start, scaled, embedding, basis, gram, held, staged, in_sem, out_sem):
-    count = gram.shape[0]
+    return jnp.concatenate(done, axis=0), jnp.concatenate(pivots, axis=0) / diagonal
+
+
+def embed_kernel(packed, start, scaled, embedding, basis, gram, held, staged, turned, in_sem, out_sem):
+    count = gram.shape[1]
     half = count // 2
-    blocks = held.shape[0]
-    block = held.shape[2]
-    reads = [
-        pltpu.make_async_copy(
-            scaled.at[:, pl.ds(b * block, block)], held.at[b], in_sem.at[b]
+    blocks, _, block = held.shape
+
+    def read(b):
+        return pltpu.make_async_copy(scaled.at[b], held.at[b], in_sem.at[b])
+
+    def write(b):
+        return pltpu.make_async_copy(
+            staged.at[:, pl.ds(b * block, block)],
+            embedding.at[:, pl.ds(b * block, block)],
+            out_sem.at[b],
         )
-        for b in range(blocks)
-    ]
-    for read in reads:
-        read.start()
+
+    for b in range(blocks):
+        read(b).start()
 
     base = 3 * half * (half // LANES)
     degree = jnp.concatenate(
@@ -239,43 +333,51 @@
             axis=1,
         )
 
-    wide = jnp.concatenate([down[:, :1]] * 1, axis=1)
-    low = corner(0) * wide[:half] * across[:, :half]
+    def fill(rows, columns, values):
+        for term, part in enumerate(split(values)):
+            gram[term, rows, columns] = part
+
+    wide = jnp.concatenate([down] * (half // LANES), axis=1)
+    first, second = slice(0, half), slice(half, count)
     side = corner(1) * wide[half:] * across[:, :half]
-    high = corner(2) * wide[half:] * across[:, half:]
-    gram[:half, :half] = low
-    gram[half:, :half] = side
-    gram[:half, half:] = jnp.transpose(side)
-    gram[half:, half:] = high
-
-    def iterate(_, turned):
-        image = dot(turned, gram[...], NN, HIGHEST)
-        square = dot(image, image, NT, HIGHEST)
-        return dot(inverse_cholesky(square), image, NN, HIGHEST)
-
-    turned = lax.fori_loop(0, ITERS, iterate, jnp.transpose(start[...]))
-    basis[...] = turned
-    weighted = (turned * across).astype(jnp.bfloat16)
-    writes = []
+    fill(first, first, corner(0) * wide[:half] * across[:, :half])
+    fill(second, first, side)
+    fill(first, second, jnp.transpose(side))
+    fill(second, second, corner(2) * wide[half:] * across[:, half:])
+
+    def advance(rows, steps):
+        for _ in range(steps):
+            rows = exact_dot(split(rows), [gram[0], gram[1], gram[2]], NN)
+        terms = split(rows)
+        inverse, ratio = inverse_cholesky(exact_dot(terms, terms, NT))
+        return exact_dot(split(inverse), terms, NN), ratio
+
+    begin = jnp.transpose(start[...])
+    rows, good = begin, None
+    for steps, least in GROUPS:
+        rows, ratio = advance(rows, steps)
+        here = jnp.where(ratio > least, 1.0, 0.0)
+        good = here if good is None else good * here
+    turned[...] = rows
+
+    @pl.when(jnp.logical_not(jnp.min(good) > 0.5))
+    def _():
+        turned[...] = lax.fori_loop(0, ITERS, lambda _, rows: advance(rows, 1)[0], begin)
+
+    basis[...] = turned[...]
+    weighted = (turned[...] * across).astype(jnp.bfloat16)
     for b in range(blocks):
-        reads[b].wait()
+        read(b).wait()
         staged[:, b * block : (b + 1) * block] = dot(weighted, held[b], NN)
-        write = pltpu.make_async_copy(
-            staged.at[:, pl.ds(b * block, block)],
-            embedding.at[:, pl.ds(b * block, block)],
-            out_sem.at[b],
-        )
-        write.start()
-        writes.append(write)
-    for write in writes:
-        write.wait()
+        write(b).start()
+    for b in range(blocks):
+        write(b).wait()
 
 
 def embed(packed, start_basis, scaled):
-    count, rows_here = scaled.shape
+    blocks, count, block = scaled.shape
     kept = start_basis.shape[1]
-    block = BLOCK
-    blocks = rows_here // block
+    rows_here = blocks * block
     return pl.pallas_call(
         embed_kernel,
         out_shape=(
@@ -292,13 +394,14 @@
             pl.BlockSpec(memory_space=pltpu.VMEM),
         ),
         scratch_shapes=[
-            pltpu.VMEM((count, count), jnp.float32),
+            pltpu.VMEM((3, count, count), jnp.bfloat16),
             pltpu.VMEM((blocks, count, block), jnp.bfloat16),
             pltpu.VMEM((kept, rows_here), jnp.float32),
+            pltpu.VMEM((kept, count), jnp.float32),
             pltpu.SemaphoreType.DMA((blocks,)),
             pltpu.SemaphoreType.DMA((blocks,)),
         ],
-        compiler_params=pltpu.CompilerParams(vmem_limit_bytes=48 * 2**20),
+        compiler_params=pltpu.CompilerParams(vmem_limit_bytes=50 * 2**20),
     )(packed, start_basis, scaled)
 
 

time: 168 us -> 170 us (1.012)
  Pallas kernels: 65 us -> 67.1 us
    pallas_call x1, Pallas kernels: 30.5 us -> 40.9 us  [embed(): pl.pallas_call(embed_kernel, out_shape=(jax.ShapeDtypeStruct((kept, rows_...]
    pallas_call x1, Pallas kernels: 30.4 us -> 22 us  [main_pass(): pl.pallas_call(main_kernel, out_shape=(jax.ShapeDtypeStruct((blocks, coun...]
where the time goes in v3:
time: 170 us
  blocking collectives  77 us (45%)
  Pallas kernels  67.1 us (39%)
  waiting for transfers between devices  19.7 us (12%)
  starting transfers between devices  3.74 us (2%)
    all_to_all x2, blocking collectives, total_over(): pieces = lax.all_to_all(pieces, axes, 0, 0, tiled=True)  54.1 us
    pallas_call x1, Pallas kernels, embed(): pl.pallas_call(embed_kernel, out_shape=(jax.ShapeDtypeStruct((kept, rows_...  40.9 us
    all_to_all x1, blocking collectives, total_over(): spread = lax.all_to_all(spread, axes, 0, 0, tiled=True)  22.9 us
    pallas_call x1, Pallas kernels, main_pass(): pl.pallas_call(main_kernel, out_shape=(jax.ShapeDtypeStruct((blocks, coun...  22 us
    all_to_all x1, waiting for transfers between devices, total_over(): spread = lax.all_to_all(spread, axes, 0, 0, tiled=True)  19.7 us
    pallas_call x1, Pallas kernels, pick(): pl.pallas_call(functools.partial(pick_kernel, axes), out_shape=jax.ShapeD...  4.16 us
    all_to_all x1, starting transfers between devices, total_over(): spread = lax.all_to_all(spread, axes, 0, 0, tiled=True)  3.74 us
  transfers between devices with their start and end apart: 1, of which 1 were waited for; matrix products, arithmetic and copies ran while one was open for 0% of the time, Pallas kernels for 0%

profile of v3, /device:TPU:1, one launch (start us, length us, event | category | flops | bytes accessed | tf_op | source)
XLA Modules:
  0.0 169.9 jit_solution(16830464616021570281)
XLA Ops:
  0.6 4.2 %shard_map.50 = f32[2048,128]{1,0:T(8,128)} custom-call(s32[512]{0:T(512)} %index.1, bf16[16384,512]{1,0:T(8,128)(2,1)} %windows.3), custom_call_target="tpu_custom_call" | custom-call | tf_op jit(solution)/shard_map/pallas_call | solution.py:78
  4.8 0.0 copy-start
  4.8 31.3 %all_to_all.20 = f32[128,16,128]{2,1,0:T(8,128)S(1)} all-to-all(f32[128,16,128]{2,1,0:T(8,128)} %bitcast.8), channel_id=1, replica_groups=mesh['rows'=32,'sub'=4] {'rows','sub'}, dimensions={0} | all-to-all | bytes 2097152 | tf_op jit(solution)/shard_map/all_to_all | solution.py:411
  36.1 0.1 reduce_sum.18
  36.2 0.1 broadcast_in_dim.4
  36.3 22.9 %all_to_all.21 = f32[128,16,128]{2,1,0:T(8,128)S(1)} all-to-all(f32[128,16,128]{2,1,0:T(8,128)S(1)} %broadcast_in_dim.4), channel_id=1, replica_groups=mesh['rows'=32,'sub'=4] {'rows','sub'}, dimensions={0} | all-to-all | bytes 2097152 | tf_op jit(solution)/shard_map/all_to_all | solution.py:414
  59.2 22.0 %shard_map.51 = (bf16[32,512,512]{2,1,0:T(8,128)(2,1)}, f32[2048,128]{1,0:T(8,128)S(1)}) custom-call(f32[2048,128]{1,0:T(8,128)S(1)} %bitcast.6, bf16[16384,512]{1,0:T(8,128)(2,1)} %windows.3), custom_call_target="tpu_custom_call" | custom-call | tf_op jit(solution)/shard_map/pallas_call | solution.py:221
  81.2 22.9 %all_to_all.22 = f32[128,16,128]{2,1,0:T(8,128)S(1)} all-to-all(f32[128,16,128]{2,1,0:T(8,128)S(1)} %bitcast.7), channel_id=1, replica_groups=mesh['rows'=32,'sub'=4] {'rows','sub'}, dimensions={0} | all-to-all | bytes 2097152 | tf_op jit(solution)/shard_map/all_to_all | solution.py:411
  104.1 0.1 reduce_sum.19
  104.2 1.0 broadcast_in_dim.5
  105.2 3.7 %all-to-all-start.3 = ((f32[128,16,128]{2,1,0:T(8,128)}), f32[128,16,128]{2,1,0:T(8,128)S(1)}, u32[]{:S(2)}, u32[]{:S(2)}) async-start(f32[128,16,128]{2,1,0:T(8,128)} %broadcast_in_dim.5), calls=%async_computation.3 | async-start | bytes 2097152 | tf_op jit(solution)/shard_map/all_to_all | solution.py:414
  109.0 0.0 copy-done
  109.0 0.1 copy.5.start
  109.1 19.7 %all-to-all-done.3 = f32[128,16,128]{2,1,0:T(8,128)S(1)} async-done(((f32[128,16,128]{2,1,0:T(8,128)}), f32[128,16,128]{2,1,0:T(8,128)S(1)}, u32[]{:S(2)}, u32[]{:S(2)}) %all-to-all-start.3) | async-done | bytes 1048608 | tf_op jit(solution)/shard_map/all_to_all | solution.py:414
  128.8 40.9 %shard_map.52 = (f32[64,16384]{1,0:T(8,128)}, f32[64,512]{1,0:T(8,128)}) custom-call(f32[2048,128]{1,0:T(8,128)S(1)} %bitcast.5, f32[512,64]{1,0:T(8,128)S(1)} %copy.5.start, bf16[32,512,512]{2,1,0:T(8,128)(2,1)} %get-tuple-element.7.scaled), custom_call_target="tpu_custom_call" | custom-call | tf_op jit(solution)/shard_map/pallas_call | solution.py:381
Async XLA Ops:
  4.8 104.2 %copy-start = (f32[512,64]{0,1:T(8,128)S(1)}, f32[512,64]{0,1:T(8,128)}, u32[]{:S(2)}) copy-start(f32[512,64]{0,1:T(8,128)} %param.5) | copy-start | bytes 393220
  105.2 23.6 %all-to-all-start.3 = ((f32[128,16,128]{2,1,0:T(8,128)}), f32[128,16,128]{2,1,0:T(8,128)S(1)}, u32[]{:S(2)}, u32[]{:S(2)}) async-start(f32[128,16,128]{2,1,0:T(8,128)} %broadcast_in_dim.5), calls=%async_computation.3 | async-start | bytes 2097152 | tf_op jit(solution)/shard_map/all_to_all | solution.py:414

commit v4 on v3

--- a/solution.py
+++ b/solution.py
@@ -2,7 +2,6 @@
 
 import jax
 import jax.numpy as jnp
-import numpy as np
 from jax import lax
 from jax.experimental import pallas as pl
 from jax.experimental.pallas import tpu as pltpu
@@ -32,11 +31,13 @@
 NT = ((1,), (1,))
 
 
-def pick_kernel(axes, index, windows, out, held, listed, sem):
+def pick_kernel(axes, index, windows, keep, send, held, listed, sem):
     count = index.shape[0]
     rows_here, width = windows.shape
     parts = width // LANES
     offset = lax.axis_index(axes) * rows_here
+    core = lax.axis_index(axes[0]) % 2
+    half = keep.shape[0]
 
     def note(j, found):
         local = index[j] - offset
@@ -63,12 +64,18 @@
         row = lax.broadcasted_iota(jnp.int32, block.shape, 0)
         here = row == (index[j] - offset) % 16
         row = jnp.sum(jnp.where(here, block, 0.0), axis=0, keepdims=True)
-        for c in range(parts):
-            out[pl.ds(parts * j + c, 1), :] = row[:, c * LANES : (c + 1) * LANES]
+        for side, out in ((core, keep), (1 - core, send)):
+
+            @pl.when((parts * j) // half == side)
+            def _():
+                for c in range(parts):
+                    out[pl.ds((parts * j) % half + c, 1), :] = row[:, c * LANES : (c + 1) * LANES]
+
         return carry
 
     lax.fori_loop(0, found, begin, 0)
-    out[...] = jnp.zeros_like(out)
+    keep[...] = jnp.zeros_like(keep)
+    send[...] = jnp.zeros_like(send)
     lax.fori_loop(0, found, finish, 0)
     lax.fori_loop(0, found, place, 0)
 
@@ -77,12 +84,14 @@
     count, width = index.shape[0], windows.shape[1]
     return pl.pallas_call(
         functools.partial(pick_kernel, axes),
-        out_shape=jax.ShapeDtypeStruct((count * width // LANES, LANES), jnp.float32),
+        out_shape=(
+            jax.ShapeDtypeStruct((count * width // LANES // 2, LANES), jnp.float32),
+        ) * 2,
         in_specs=[
             pl.BlockSpec(memory_space=pltpu.SMEM),
             pl.BlockSpec(memory_space=pl.ANY),
         ],
-        out_specs=pl.BlockSpec(memory_space=pltpu.VMEM),
+        out_specs=(pl.BlockSpec(memory_space=pltpu.VMEM),) * 2,
         scratch_shapes=[
             pltpu.VMEM((count, 16, width), jnp.bfloat16),
             pltpu.SMEM((count + 1,), jnp.int32),
@@ -93,8 +102,9 @@
 
 
 def main_kernel(
-    marks, windows, scaled, packed, land, land_scale, held, made, products, cross, column, in_sem, out_sem
+    axis, own, other, windows, scaled, keep, send, land, land_scale, held, made, products, cross, column, in_sem, out_sem
 ):
+    core = lax.axis_index(axis) % 2
     count, width = land.shape
     half = count // 2
     parts = width // LANES
@@ -114,15 +124,17 @@
 
     lax.fori_loop(0, blocks, begin, 0)
 
-    square = jnp.zeros((count, 1), jnp.float32)
-    for c in range(parts):
-        piece = marks[pl.ds(c, count, stride=parts), :]
-        land[:, c * LANES : (c + 1) * LANES] = piece.astype(jnp.bfloat16)
-        square += jnp.sum(piece * piece, axis=1, keepdims=True)
-    inverse = lax.rsqrt(square / width + epsilon)
-    land_scale[...] = jnp.broadcast_to(
-        inverse * (sharpness * LOG2E / width), land_scale.shape
-    )
+    for side, marks in ((core, own), (1 - core, other)):
+        here = pl.ds(pl.multiple_of(side * half, half), half)
+        square = jnp.zeros((half, 1), jnp.float32)
+        for c in range(parts):
+            piece = marks[pl.ds(c, half, stride=parts), :]
+            land[here, c * LANES : (c + 1) * LANES] = piece.astype(jnp.bfloat16)
+            square += jnp.sum(piece * piece, axis=1, keepdims=True)
+        inverse = lax.rsqrt(square / width + epsilon)
+        land_scale[here, :] = jnp.broadcast_to(
+            inverse * (sharpness * LOG2E / width), (half, LANES)
+        )
     cross[...] = jnp.zeros_like(cross)
     column[...] = jnp.zeros_like(column)
     made[0] = jnp.zeros(made.shape[1:], made.dtype)
@@ -195,16 +207,27 @@
     lax.fori_loop(0, blocks // UNROLL, several, 0)
     gather(blocks - 1)
 
-    packed[...] = jnp.zeros_like(packed)
+    keep[...] = jnp.zeros_like(keep)
+    send[...] = jnp.zeros_like(send)
+
+    def place(at, values):
+        which, row = divmod(at, keep.shape[0])
+        for side, out in ((core, keep), (1 - core, send)):
+
+            @pl.when(side == which)
+            def _():
+                out[row : row + values.shape[0], :] = values
+
     at = 0
     for b in range(3):
         for c in range(half // LANES):
-            packed[at : at + half, :] = cross[b, :, c * LANES : (c + 1) * LANES]
+            place(at, cross[b, :, c * LANES : (c + 1) * LANES])
             at += half
+    degrees = []
     for c in range(count // LANES):
         turned = jnp.transpose(column[c * LANES : (c + 1) * LANES, :])
-        packed[at : at + 1, :] = jnp.sum(turned, axis=0, keepdims=True)
-        at += 1
+        degrees.append(jnp.sum(turned, axis=0, keepdims=True))
+    place(at, jnp.concatenate(degrees, axis=0))
 
     def finish(b, carry):
         write(b).wait()
@@ -213,23 +236,26 @@
     lax.fori_loop(0, blocks, finish, 0)
 
 
-def main_pass(marks, windows, total_rows):
+def main_pass(own, other, windows, total_rows, axis):
     rows_here, width = windows.shape
-    count = marks.shape[0] * LANES // width
+    count = 2 * own.shape[0] * LANES // width
     half = count // 2
     blocks = rows_here // SUB
     return pl.pallas_call(
-        main_kernel,
+        functools.partial(main_kernel, axis),
         out_shape=(
             jax.ShapeDtypeStruct((blocks, count, SUB), jnp.bfloat16),
-            jax.ShapeDtypeStruct((total_rows, LANES), jnp.float32),
+            jax.ShapeDtypeStruct((total_rows // 2, LANES), jnp.float32),
+            jax.ShapeDtypeStruct((total_rows // 2, LANES), jnp.float32),
         ),
         in_specs=[
             pl.BlockSpec(memory_space=pltpu.VMEM),
+            pl.BlockSpec(memory_space=pltpu.VMEM),
             pl.BlockSpec(memory_space=pl.ANY),
         ],
         out_specs=(
             pl.BlockSpec(memory_space=pl.ANY),
+            pl.BlockSpec(memory_space=pltpu.VMEM),
             pl.BlockSpec(memory_space=pltpu.VMEM),
         ),
         scratch_shapes=[
@@ -244,7 +270,7 @@
             pltpu.SemaphoreType.DMA((blocks,)),
         ],
         compiler_params=pltpu.CompilerParams(vmem_limit_bytes=44 * 2**20),
-    )(marks, windows)
+    )(own, other, windows)
 
 
 def split(values):
@@ -293,7 +319,10 @@
     return jnp.concatenate(done, axis=0), jnp.concatenate(pivots, axis=0) / diagonal
 
 
-def embed_kernel(packed, start, scaled, embedding, basis, gram, held, staged, turned, in_sem, out_sem):
+def embed_kernel(
+    axis, own, other, start, scaled, embedding, basis, packed, gram, held, staged, turned, in_sem, out_sem
+):
+    core = lax.axis_index(axis) % 2
     count = gram.shape[1]
     half = count // 2
     blocks, _, block = held.shape
@@ -311,6 +340,9 @@
     for b in range(blocks):
         read(b).start()
 
+    size = own.shape[0]
+    packed[pl.ds(pl.multiple_of(core * size, size), size), :] = own[...]
+    packed[pl.ds(pl.multiple_of((1 - core) * size, size), size), :] = other[...]
     base = 3 * half * (half // LANES)
     degree = jnp.concatenate(
         [packed[base + c : base + c + 1, :] for c in range(count // LANES)], axis=1
@@ -374,12 +406,12 @@
         write(b).wait()
 
 
-def embed(packed, start_basis, scaled):
+def embed(own, other, start_basis, scaled, axis):
     blocks, count, block = scaled.shape
     kept = start_basis.shape[1]
     rows_here = blocks * block
     return pl.pallas_call(
-        embed_kernel,
+        functools.partial(embed_kernel, axis),
         out_shape=(
             jax.ShapeDtypeStruct((kept, rows_here), jnp.float32),
             jax.ShapeDtypeStruct((kept, count), jnp.float32),
@@ -387,6 +419,7 @@
         in_specs=[
             pl.BlockSpec(memory_space=pltpu.VMEM),
             pl.BlockSpec(memory_space=pltpu.VMEM),
+            pl.BlockSpec(memory_space=pltpu.VMEM),
             pl.BlockSpec(memory_space=pl.ANY),
         ],
         out_specs=(
@@ -394,6 +427,7 @@
             pl.BlockSpec(memory_space=pltpu.VMEM),
         ),
         scratch_shapes=[
+            pltpu.VMEM((2 * own.shape[0], LANES), jnp.float32),
             pltpu.VMEM((3, count, count), jnp.bfloat16),
             pltpu.VMEM((blocks, count, block), jnp.bfloat16),
             pltpu.VMEM((kept, rows_here), jnp.float32),
@@ -402,33 +436,44 @@
             pltpu.SemaphoreType.DMA((blocks,)),
         ],
         compiler_params=pltpu.CompilerParams(vmem_limit_bytes=50 * 2**20),
-    )(packed, start_basis, scaled)
-
-
-def total_over(values, axes, devices):
-    rows = values.shape[0] // devices
-    pieces = values.reshape(devices, rows, LANES)
-    pieces = lax.all_to_all(pieces, axes, 0, 0, tiled=True)
+    )(own, other, start_basis, scaled)
+
+
+def total_over(keep, send, axes, shape):
+    rows, sub = shape
+    chips = rows // 2 * sub
+    cores = [(r, r ^ 1) for r in range(rows)]
+    groups = [
+        [r * sub + s for r in range(c, rows, 2) for s in range(sub)] for c in range(2)
+    ]
+
+    def exchange(values):
+        return lax.all_to_all(
+            values, axes, 0, 0, axis_index_groups=groups, tiled=True
+        )
+
+    values = keep + lax.ppermute(send, axes[0], cores)
+    pieces = exchange(values.reshape(chips, keep.shape[0] // chips, LANES))
     mine = jnp.sum(pieces, axis=0)
-    spread = jnp.broadcast_to(mine[None], pieces.shape)
-    spread = lax.all_to_all(spread, axes, 0, 0, tiled=True)
-    return spread.reshape(values.shape)
-
-
-def per_device(devices, windows, landmark_index, start_basis):
+    own = exchange(jnp.broadcast_to(mine[None], pieces.shape)).reshape(keep.shape)
+    return own, lax.ppermute(own, axes[0], cores)
+
+
+def per_device(shape, windows, landmark_index, start_basis):
     axes = ("rows", "sub")
-    marks = total_over(pick(landmark_index, windows, axes), axes, devices)
-    scaled, packed = main_pass(marks, windows, devices * CHUNK)
-    packed = total_over(packed, axes, devices)
-    embedding, turned = embed(packed, start_basis, scaled)
+    own, other = total_over(*pick(landmark_index, windows, axes), axes, shape)
+    total_rows = shape[0] * shape[1] * CHUNK
+    scaled, keep, send = main_pass(own, other, windows, total_rows, axes[0])
+    own, other = total_over(keep, send, axes, shape)
+    embedding, turned = embed(own, other, start_basis, scaled, axes[0])
     return embedding, turned.T
 
 
 def solution(mesh):
     placed = (P(("rows", "sub"), None), P(), P())
-    devices = int(np.prod(list(mesh.shape.values())))
+    shape = (mesh.shape["rows"], mesh.shape["sub"])
     return jax.shard_map(
-        functools.partial(per_device, devices),
+        functools.partial(per_device, shape),
         mesh=mesh,
         in_specs=placed,
         out_specs=(P(None, ("rows", "sub")), P()),

time: 170 us -> 155 us (0.912)
  waiting for transfers between devices: 19.7 us -> 6.23 us
  blocking collectives: 77 us -> 70.8 us
  starting transfers between devices: 3.74 us -> 8.51 us
    all_to_all x1 -> x0, waiting for transfers between devices: 19.7 us -> none  [total_over(): spread = lax.all_to_all(spread, axes, 0, 0, tiled=True)]
    ppermute x0 -> x4, starting transfers between devices: none -> 8.51 us  [the longest x2 6.54 us: total_over(): return (own, lax.ppermute(own, axes[0], cores))]
    all_to_all x3 -> x4, blocking collectives: 77 us -> 70.8 us  [exchange(): lax.all_to_all(values, axes, 0, 0, axis_index_groups=groups, tiled=True)]
    ppermute x0 -> x4, waiting for transfers between devices: none -> 6.23 us  [the longest x2 3.28 us: total_over(): values = keep + lax.ppermute(send, axes[0], cores)]
    all_to_all x1 -> x0, starting transfers between devices: 3.74 us -> none  [total_over(): spread = lax.all_to_all(spread, axes, 0, 0, tiled=True)]
  transfers between devices with their start and end apart: 1 -> 4, of which waited for: 1 -> 4; matrix products, arithmetic and copies ran while one was open for 0% -> 0% of each run, Pallas kernels for 0% -> 0%
where the time goes in v4:
time: 155 us
  blocking collectives  70.8 us (46%)
  Pallas kernels  67 us (43%)
  starting transfers between devices  8.51 us (5%)
  waiting for transfers between devices  6.23 us (4%)
    all_to_all x4, blocking collectives, exchange(): lax.all_to_all(values, axes, 0, 0, axis_index_groups=groups, tiled=True)  70.8 us
    pallas_call x1, Pallas kernels, embed(): pl.pallas_call(functools.partial(embed_kernel, axis), out_shape=(jax.Shap...  41 us
    pallas_call x1, Pallas kernels, main_pass(): pl.pallas_call(functools.partial(main_kernel, axis), out_shape=(jax.Shape...  21.8 us
    ppermute x2, starting transfers between devices, total_over(): return (own, lax.ppermute(own, axes[0], cores))  6.54 us
    pallas_call x1, Pallas kernels, pick(): pl.pallas_call(functools.partial(pick_kernel, axes), out_shape=(jax.Shape...  4.14 us
    ppermute x2, waiting for transfers between devices, total_over(): values = keep + lax.ppermute(send, axes[0], cores)  3.28 us
  transfers between devices with their start and end apart: 4, of which 4 were waited for; matrix products, arithmetic and copies ran while one was open for 0% of the time, Pallas kernels for 0%

profile of v4, /device:TPU:1, one launch (start us, length us, event | category | flops | bytes accessed | tf_op | source)
XLA Modules:
  0.0 155.0 jit_solution(15827624702616448049)
XLA Ops:
  0.6 4.1 %shard_map.50 = (f32[1024,128]{1,0:T(8,128)}, f32[1024,128]{1,0:T(8,128)}) custom-call(s32[512]{0:T(512)} %index.1, bf16[16384,512]{1,0:T(8,128)(2,1)} %windows.3), custom_call_target="tpu_custom_call" | custom-call | tf_op jit(solution)/shard_map/pallas_call | solution.py:85
  4.8 0.0 copy-start
  4.8 1.5 collective-permute-start
  6.3 1.7 %collective-permute-done = f32[1024,128]{1,0:T(8,128)S(1)} collective-permute-done((f32[1024,128]{1,0:T(8,128)}, f32[1024,128]{1,0:T(8,128)S(1)}, u32[]{:S(2)}, u32[]{:S(2)}) %collective-permute-start) | collective-permute-done | bytes 524320 | tf_op jit(solution)/shard_map/ppermute | solution.py:455
  8.0 1.1 add.6
  9.2 23.4 %all_to_all.20 = f32[64,16,128]{2,1,0:T(8,128)S(1)} all-to-all(f32[64,16,128]{2,1,0:T(8,128)S(1)} %bitcast.9), channel_id=1, replica_groups={{0,1,2,3,8,9,10,11,16,17,18,19,24,25,26,27,32,33,34,35,40,41,42,43,48,4..., dimensions={0} | all-to-all | bytes 1048576 | tf_op jit(solution)/shard_map/all_to_all | solution.py:451
  32.5 0.1 reduce_sum.18
  32.7 15.4 %all_to_all.21 = f32[64,16,128]{2,1,0:T(8,128)S(1)} all-to-all(f32[64,16,128]{2,1,0:T(8,128)S(1)} %broadcast_in_dim.4), channel_id=1, replica_groups={{0,1,2,3,8,9,10,11,16,17,18,19,24,25,26,27,32,33,34,35,40,41,42,43,48,4..., dimensions={0} | all-to-all | bytes 1048576 | tf_op jit(solution)/shard_map/all_to_all | solution.py:451
  48.1 3.3 %collective-permute-start.1 = (f32[1024,128]{1,0:T(8,128)S(1)}, f32[1024,128]{1,0:T(8,128)S(1)}, u32[]{:S(2)}, u32[]{:S(2)}) collective-permute-start(f32[1024,128]{1,0:T(8,128)S(1)} %bitcast.7), channel_id=1, source_target_pairs={{0,4},{4,0},{8,12},{12,8},{16,20},{20,16},{24,28},{28,24},{32,36},... | collective-permute-start | bytes 1572872 | tf_op jit(solution)/shard_map/ppermute | solution.py:459
  51.3 1.5 collective-permute-done.1.other
  52.9 21.8 %shard_map.51 = (bf16[32,512,512]{2,1,0:T(8,128)(2,1)}, f32[1024,128]{1,0:T(8,128)S(1)}, f32[1024,128]{1,0:T(8,128)S(1)}) custom-call(f32[1024,128]{1,0:T(8,128)S(1)} %bitcast.8, f32[1024,128]{1,0:T(8,128)S(1)} %collective-permute-done.1.other, bf16[16384,512]{1,0:T(8,128)(2,1)} %windows.3), custom_call_target="tpu_custom_call" | custom-call | tf_op jit(solution)/shard_map/pallas_call | solution.py:244
  74.7 0.5 collective-permute-start.2
  75.2 1.5 collective-permute-done.2
  76.7 0.1 add.7
  76.8 16.6 %all_to_all.22 = f32[64,16,128]{2,1,0:T(8,128)S(1)} all-to-all(f32[64,16,128]{2,1,0:T(8,128)S(1)} %bitcast.10), channel_id=1, replica_groups={{0,1,2,3,8,9,10,11,16,17,18,19,24,25,26,27,32,33,34,35,40,41,42,43,48,4..., dimensions={0} | all-to-all | bytes 1048576 | tf_op jit(solution)/shard_map/all_to_all | solution.py:451
  93.4 0.1 reduce_sum.19
  93.5 15.4 %all_to_all.23 = f32[64,16,128]{2,1,0:T(8,128)S(1)} all-to-all(f32[64,16,128]{2,1,0:T(8,128)S(1)} %broadcast_in_dim.5), channel_id=1, replica_groups={{0,1,2,3,8,9,10,11,16,17,18,19,24,25,26,27,32,33,34,35,40,41,42,43,48,4..., dimensions={0} | all-to-all | bytes 1048576 | tf_op jit(solution)/shard_map/all_to_all | solution.py:451
  109.0 3.3 %collective-permute-start.3 = (f32[1024,128]{1,0:T(8,128)S(1)}, f32[1024,128]{1,0:T(8,128)S(1)}, u32[]{:S(2)}, u32[]{:S(2)}) collective-permute-start(f32[1024,128]{1,0:T(8,128)S(1)} %bitcast.5), channel_id=1, source_target_pairs={{0,4},{4,0},{8,12},{12,8},{16,20},{20,16},{24,28},{28,24},{32,36},... | collective-permute-start | bytes 1572872 | tf_op jit(solution)/shard_map/ppermute | solution.py:459
  112.2 0.0 copy-done
  112.2 0.1 copy.5.start
  112.4 1.4 collective-permute-done.3.other
  113.8 41.0 %shard_map.52 = (f32[64,16384]{1,0:T(8,128)}, f32[64,512]{1,0:T(8,128)}) custom-call(f32[1024,128]{1,0:T(8,128)S(1)} %bitcast.6, f32[1024,128]{1,0:T(8,128)S(1)} %collective-permute-done.3.other, f32[512,64]{1,0:T(8,128)S(1)} %copy.5.start, bf16[32,512,512]{2,1,0:T(8,128)(2,1)} %get-tuple-element.13.scaled), custom_call_target="tpu_custom_call" | custom-call | tf_op jit(solution)/shard_map/pallas_call | solution.py:413
  (2 shorter events, 0.1 us)
Async XLA Ops:
  4.8 107.5 %copy-start = (f32[512,64]{0,1:T(8,128)S(1)}, f32[512,64]{0,1:T(8,128)}, u32[]{:S(2)}) copy-start(f32[512,64]{0,1:T(8,128)} %param.5) | copy-start | bytes 393220
  4.8 3.3 %collective-permute-start = (f32[1024,128]{1,0:T(8,128)}, f32[1024,128]{1,0:T(8,128)S(1)}, u32[]{:S(2)}, u32[]{:S(2)}) collective-permute-start(f32[1024,128]{1,0:T(8,128)} %get-tuple-element.10), channel_id=1, source_target_pairs={{0,4},{4,0},{8,12},{12,8},{16,20},{20,16},{24,28},{28,24},{32,36},... | collective-permute-start | bytes 1572872 | tf_op jit(solution)/shard_map/ppermute | solution.py:455
  48.1 4.8 %collective-permute-start.1 = (f32[1024,128]{1,0:T(8,128)S(1)}, f32[1024,128]{1,0:T(8,128)S(1)}, u32[]{:S(2)}, u32[]{:S(2)}) collective-permute-start(f32[1024,128]{1,0:T(8,128)S(1)} %bitcast.7), channel_id=1, source_target_pairs={{0,4},{4,0},{8,12},{12,8},{16,20},{20,16},{24,28},{28,24},{32,36},... | collective-permute-start | bytes 1572872 | tf_op jit(solution)/shard_map/ppermute | solution.py:459
  74.7 2.0 %collective-permute-start.2 = (f32[1024,128]{1,0:T(8,128)S(1)}, f32[1024,128]{1,0:T(8,128)S(1)}, u32[]{:S(2)}, u32[]{:S(2)}) collective-permute-start(f32[1024,128]{1,0:T(8,128)S(1)} %get-tuple-element.12), channel_id=1, source_target_pairs={{0,4},{4,0},{8,12},{12,8},{16,20},{20,16},{24,28},{28,24},{32,36},... | collective-permute-start | bytes 1572872 | tf_op jit(solution)/shard_map/ppermute | solution.py:455
  109.0 4.8 %collective-permute-start.3 = (f32[1024,128]{1,0:T(8,128)S(1)}, f32[1024,128]{1,0:T(8,128)S(1)}, u32[]{:S(2)}, u32[]{:S(2)}) collective-permute-start(f32[1024,128]{1,0:T(8,128)S(1)} %bitcast.5), channel_id=1, source_target_pairs={{0,4},{4,0},{8,12},{12,8},{16,20},{20,16},{24,28},{28,24},{32,36},... | collective-permute-start | bytes 1572872 | tf_op jit(solution)/shard_map/ppermute | solution.py:459
